TPU v7x, 32 devices: a whole 2x2x4 slice. The times are simulated.
32 devices in a mesh: seq: 8 (over z, y), head: 4 (over x, core).
Axes of the slice: x: 2, y: 2, z: 4, core: 2. Of those that a mesh axis runs over, the one named last changes fastest.
Arguments:
- query_proj: bfloat16 [2048, 2048], P('seq', 'head'), may hold values from -40 to 40
- key_proj: bfloat16 [2048, 2048], P('seq', 'head'), may hold values from -40 to 40
- value_proj: bfloat16 [2048, 4096], P('seq', 'head'), may hold values from -40 to 40
- gate_proj: bfloat16 [2048, 4096], P('seq', 'head'), may hold values from -6 to 6
- strength: float32 [32, 2048], P('head', 'seq'), may hold values from 0 to 2, as said below
- log_decay: float32 [32, 2048], P('head', 'seq'), may hold values from -1 to 0, as said below
- conv_query: bfloat16 [4, 2048], P(None, 'head'), may hold values from -3 to 3
- conv_key: bfloat16 [4, 2048], P(None, 'head'), may hold values from -3 to 3
- conv_value: bfloat16 [4, 4096], P(None, 'head'), may hold values from -3 to 3
- norm_gain: bfloat16 [128], replicated, may hold values from 0.099609375 to 1.8984375
- out_weight: bfloat16 [4096, 2048], P('head'), may hold values from -0.09375 to 0.09375
Outputs:
- layer_out: bfloat16 [2048, 2048], P(('seq', 'head'))
Inputs may be any that keep to these rules, and one draw needn't show every extreme that they name: `strength`: strictly inside the range. `log_decay`: strictly below the upper end.
All inputs are finite; a program needn't handle non-finite values.
Results may differ from a plain program's by a relative error of at most 0.014.
Values may be sent and summed in bfloat16 or wider, within the bound.
A program may use at most 64 MiB of HBM per device.

v0:
```python
import jax
import jax.numpy as jnp
from jax import lax
from jax.sharding import PartitionSpec as P

DK = 128
DV = 128
SPAN = 128


epsilon = 1e-06
highest = lax.Precision.HIGHEST


def shifted(array, axis, by):
    length = lax.axis_size(axis)
    pairs = [(i, i + by) for i in range(length) if 0 <= i + by < length]
    return lax.ppermute(array, axis, pairs)


def conv_silu(signal, before, weights):
    length = signal.shape[0]
    padded = jnp.concatenate([before, signal], axis=0).astype(jnp.float32)
    conv_taps = weights.astype(jnp.float32)
    summed = jnp.zeros(signal.shape, jnp.float32)
    for offset in range(conv_taps.shape[0]):
        summed = summed + conv_taps[offset] * padded[offset : offset + length]
    return jax.nn.silu(summed)


def apply_map(matrix, state_now):
    return jnp.einsum("hrke,hrev->hrkv", matrix, state_now, precision=highest)


def shards(
    query_proj,
    key_proj,
    value_proj,
    gate_proj,
    strength,
    log_decay,
    conv_query,
    conv_key,
    conv_value,
    norm_gain,
    out_weight,
):
    local_rows = query_proj.shape[0]
    rim_width = conv_query.shape[0] - 1
    before_query, before_key, before_value = shifted(
        (
            query_proj[local_rows - rim_width :],
            key_proj[local_rows - rim_width :],
            value_proj[local_rows - rim_width :],
        ),
        "seq",
        1,
    )
    key_heads = key_proj.shape[1] // DK
    value_heads = value_proj.shape[1] // DV
    ratio_heads = value_heads // key_heads
    spans = local_rows // SPAN
    queries = conv_silu(query_proj, before_query, conv_query)
    key_rows = conv_silu(key_proj, before_key, conv_key).reshape(local_rows, key_heads, DK)
    key_rows = key_rows / jnp.sqrt(jnp.sum(key_rows * key_rows, axis=-1, keepdims=True) + epsilon)
    values = conv_silu(value_proj, before_value, conv_value)
    query_blocks = queries.reshape(spans, SPAN, key_heads, DK).transpose(2, 0, 1, 3)[:, None]
    key_blocks = key_rows.reshape(spans, SPAN, key_heads, DK).transpose(2, 0, 1, 3)[:, None]
    value_blocks = values.reshape(spans, SPAN, key_heads, ratio_heads, DV).transpose(2, 3, 0, 1, 4)
    strength_blocks = strength.reshape(key_heads, ratio_heads, spans, SPAN)
    decay_blocks = log_decay.reshape(key_heads, ratio_heads, spans, SPAN)
    cumulative = jnp.cumsum(decay_blocks, axis=-1)
    positions = jnp.arange(SPAN)
    inclusive = positions[:, None] >= positions[None, :]
    strictly = positions[:, None] > positions[None, :]
    log_gaps = cumulative[..., :, None] - cumulative[..., None, :]
    decays = jnp.where(inclusive, jnp.exp(jnp.where(inclusive, log_gaps, 0.0)), 0.0)
    key_key = jnp.einsum("hxnck,hxnek->hxnce", key_blocks, key_blocks, precision=highest)
    query_key = jnp.einsum("hxnck,hxnek->hxnce", query_blocks, key_blocks, precision=highest)
    lower_part = jnp.where(strictly, strength_blocks[..., None] * decays * key_key, 0.0)
    system = lower_part + jnp.eye(SPAN, dtype=jnp.float32)
    right_side = jnp.concatenate(
        [
            strength_blocks[..., None] * value_blocks,
            (strength_blocks * jnp.exp(cumulative))[..., None] * key_blocks,
        ],
        axis=-1,
    )
    solved = lax.linalg.triangular_solve(
        system, right_side, left_side=True, lower=True, unit_diagonal=True
    )
    value_part = solved[..., :DV]
    key_part = solved[..., DV:]
    attention = decays * query_key
    local_out = jnp.einsum("hrnce,hrnev->hrncv", attention, value_part, precision=highest)
    coupling = jnp.exp(cumulative)[..., None] * query_blocks - jnp.einsum(
        "hrnce,hrnek->hrnck", attention, key_part, precision=highest
    )
    span_end = cumulative[..., -1:]
    scaled_keys = jnp.exp(span_end - cumulative)[..., None] * key_blocks
    transit = jnp.exp(span_end)[..., None] * jnp.eye(DK, dtype=jnp.float32) - jnp.einsum(
        "hrnck,hrnce->hrnke", scaled_keys, key_part, precision=highest
    )
    inject = jnp.einsum("hrnck,hrncv->hrnkv", scaled_keys, value_part, precision=highest)
    transit_seq = jnp.moveaxis(transit, 2, 0)
    inject_seq = jnp.moveaxis(inject, 2, 0)
    identity = jnp.broadcast_to(jnp.eye(DK, dtype=jnp.float32), (key_heads, ratio_heads, DK, DK))
    zero_state = jnp.zeros((key_heads, ratio_heads, DK, DV), jnp.float32)

    def sweep_spans(carried, span_in):
        prefix, state_now = carried
        transit_now, inject_now = span_in
        return (
            (apply_map(transit_now, prefix), apply_map(transit_now, state_now) + inject_now),
            (prefix, state_now),
        )

    (total_map, local_end), (prefixes, starts) = lax.scan(
        sweep_spans, (identity, zero_state), (transit_seq, inject_seq)
    )
    partial_out = local_out + jnp.einsum(
        "hrnck,hrnkv->hrncv", coupling, jnp.moveaxis(starts, 0, 2), precision=highest
    )
    reach_map = jnp.einsum(
        "hrnck,hrnke->hrnce", coupling, jnp.moveaxis(prefixes, 0, 2), precision=highest
    )

    def relay_step(hop_index, state_now):
        return shifted(apply_map(total_map, state_now) + local_end, "seq", 1)

    incoming = lax.fori_loop(0, lax.axis_size("seq") - 1, relay_step, zero_state)
    core_out = partial_out + jnp.einsum("hrnce,hrev->hrncv", reach_map, incoming, precision=highest)
    core_out = core_out.transpose(2, 3, 0, 1, 4).reshape(local_rows, value_heads, DV)
    gate_values = gate_proj.astype(jnp.float32).reshape(local_rows, value_heads, DV)
    scale_rows = lax.rsqrt(jnp.mean(core_out * core_out, axis=-1, keepdims=True) + epsilon)
    normed = core_out * scale_rows * norm_gain.astype(jnp.float32) * jax.nn.silu(gate_values)
    hidden = normed.reshape(local_rows, value_heads * DV).astype(jnp.bfloat16)
    return lax.psum_scatter(
        jnp.dot(hidden, out_weight, preferred_element_type=jnp.float32).astype(jnp.bfloat16),
        "head",
        scatter_dimension=0,
        tiled=True,
    )


def solution(mesh):
    placed = (
        P("seq", "head"),
        P("seq", "head"),
        P("seq", "head"),
        P("seq", "head"),
        P("head", "seq"),
        P("head", "seq"),
        P(None, "head"),
        P(None, "head"),
        P(None, "head"),
        P(),
        P("head", None),
    )
    return jax.shard_map(
        shards, mesh=mesh, in_specs=placed, out_specs=P(("seq", "head"), None), check_vma=False
    )
```

profile of v0, /device:TPU:29, one launch (start us, length us, event | category | flops | bytes accessed | tf_op | source)
XLA Modules:
  0.0 358.9 jit_solution(8311823938647776074)
XLA Ops:
  6.5 0.7 slice.113
  7.3 1.3 collective-permute-start.3
  9.3 1.3 collective-permute-start.2
  11.2 1.3 collective-permute-start.1
  12.6 0.7 reshape.128
  13.3 2.4 reduce_window_sum.11
  16.0 0.9 fusion.80
  16.9 0.7 mul.314
  17.6 0.8 fusion.82
  18.5 0.8 fusion.81
  20.3 1.0 maximum_convert_fusion.2
  22.8 1.2 fusion.83
  25.2 1.2 fusion.78
  26.4 0.8 copy.110
  27.3 157.9 %custom-call.3 = f32[4,2,2,1,128,128]{4,5,3,2,1,0:T(8,128)} custom-call(f32[4,2,2,1,128,128]{5,4,3,2,1,0:T(8,128)S(1)} %select_add_fusion), custom_call_target="InvertDiagBlocksLowerTriangular" | custom-call | tf_op jit(solution)/shard_map/triangular_solve | solution.py:89
  185.1 1.2 maximum_convert_fusion
  186.9 1.9 reshape.131
  188.8 2.0 bitcast_multiply_fusion.1
  190.9 2.0 fusion.11
  192.9 3.2 fusion.41
  196.1 3.2 fusion.25
  199.3 2.2 fusion.22
  201.6 5.0 %while.28 = (s32[]{:T(128)}, f32[4,2,128,128]{3,2,1,0:T(8,128)S(1)}, f32[4,2,128,128]{3,2,1,0:T(8,128)S(1)}, f32[2,4,2,128,128]{4,3,2,1,0:T(8,128)}, f32[2,4,2,1...) while((s32[]{:T(128)}, ...), condition=%wide.region_3.4_spmd.clone, body=%wide.region_2.3_spmd.clone.sunk | while | flops 403046400 | bytes 12060307 | solution.py:118
  201.7 1.1 bitcast_dynamic-update-slice_fusion.3
  204.2 1.1 bitcast_dynamic-update-slice_fusion.3
  206.6 3.1 convolution_subtract_fusion
  209.8 1.2 fusion.39
  211.3 2.9 convolution_add_fusion.3
  214.2 94.3 %while.27 = (s32[]{:T(128)}, f32[4,2,128,128]{3,2,1,0:T(8,128)S(1)}, f32[4,2,128,128]{3,2,1,0:T(8,128)S(1)}, f32[4,2,128,128]{3,2,1,0:T(8,128)S(1)}, s32[]{:T(128)}) while((s32[]{:T(128)}, f32[4,2,128,128]{3,2,1,0:T(8,128)S(1)}, f32[4,2,128,128]{3,2,1,0:T(8,128)S(1)}, f32[4,2,128,128]{3,2,1,0:T(8,128)S(1)}, s32[]{:T(128)}) %tuple.61), condition=%wide.region_5.6_spmd, body=%wide.region_4.5_spmd.sunk | while | flops 201457664 | bytes 4194405 | solution.py:131
  214.9 1.3 collective-permute-start
  216.2 15.3 %collective-permute-done = f32[4,2,128,128]{3,2,1,0:T(8,128)S(1)} collective-permute-done((f32[4,2,128,128]{3,2,1,0:T(8,128)S(1)}, f32[4,2,128,128]{3,2,1,0:T(8,128)S(1)}, u32[]{:S(2)}, u32[]{:S(2)}) %collective-permute-start) | collective-permute-done | bytes 524320 | tf_op jit(solution)/shard_map/while/body/eval_jaxpr/ppermute | solution.py:18
  232.1 1.3 collective-permute-start
  233.4 13.0 %collective-permute-done = f32[4,2,128,128]{3,2,1,0:T(8,128)S(1)} collective-permute-done((f32[4,2,128,128]{3,2,1,0:T(8,128)S(1)}, f32[4,2,128,128]{3,2,1,0:T(8,128)S(1)}, u32[]{:S(2)}, u32[]{:S(2)}) %collective-permute-start) | collective-permute-done | bytes 524320 | tf_op jit(solution)/shard_map/while/body/eval_jaxpr/ppermute | solution.py:18
  247.1 1.3 collective-permute-start
  248.4 12.1 %collective-permute-done = f32[4,2,128,128]{3,2,1,0:T(8,128)S(1)} collective-permute-done((f32[4,2,128,128]{3,2,1,0:T(8,128)S(1)}, f32[4,2,128,128]{3,2,1,0:T(8,128)S(1)}, u32[]{:S(2)}, u32[]{:S(2)}) %collective-permute-start) | collective-permute-done | bytes 524320 | tf_op jit(solution)/shard_map/while/body/eval_jaxpr/ppermute | solution.py:18
  261.1 1.3 collective-permute-start
  262.4 11.2 %collective-permute-done = f32[4,2,128,128]{3,2,1,0:T(8,128)S(1)} collective-permute-done((f32[4,2,128,128]{3,2,1,0:T(8,128)S(1)}, f32[4,2,128,128]{3,2,1,0:T(8,128)S(1)}, u32[]{:S(2)}, u32[]{:S(2)}) %collective-permute-start) | collective-permute-done | bytes 524320 | tf_op jit(solution)/shard_map/while/body/eval_jaxpr/ppermute | solution.py:18
  274.3 1.3 collective-permute-start
  275.6 10.3 %collective-permute-done = f32[4,2,128,128]{3,2,1,0:T(8,128)S(1)} collective-permute-done((f32[4,2,128,128]{3,2,1,0:T(8,128)S(1)}, f32[4,2,128,128]{3,2,1,0:T(8,128)S(1)}, u32[]{:S(2)}, u32[]{:S(2)}) %collective-permute-start) | collective-permute-done | bytes 524320 | tf_op jit(solution)/shard_map/while/body/eval_jaxpr/ppermute | solution.py:18
  286.5 1.3 collective-permute-start
  287.8 9.2 %collective-permute-done = f32[4,2,128,128]{3,2,1,0:T(8,128)S(1)} collective-permute-done((f32[4,2,128,128]{3,2,1,0:T(8,128)S(1)}, f32[4,2,128,128]{3,2,1,0:T(8,128)S(1)}, u32[]{:S(2)}, u32[]{:S(2)}) %collective-permute-start) | collective-permute-done | bytes 524320 | tf_op jit(solution)/shard_map/while/body/eval_jaxpr/ppermute | solution.py:18
  297.7 1.3 collective-permute-start
  299.0 9.5 %collective-permute-done = f32[4,2,128,128]{3,2,1,0:T(8,128)S(1)} collective-permute-done((f32[4,2,128,128]{3,2,1,0:T(8,128)S(1)}, f32[4,2,128,128]{3,2,1,0:T(8,128)S(1)}, u32[]{:S(2)}, u32[]{:S(2)}) %collective-permute-start) | collective-permute-done | bytes 524320 | tf_op jit(solution)/shard_map/while/body/eval_jaxpr/ppermute | solution.py:18
  308.5 2.4 multiply_reduce_fusion
  310.9 0.8 copy.78
  311.7 0.8 reshape.132
  313.1 4.6 %convolution_convert_fusion = bf16[256,2048]{1,0:T(8,128)(2,1)} fusion(bf16[1024,2048]{1,0:T(8,128)(2,1)} %param.25, bf16[256,1024]{1,0:T(8,128)(2,1)S(1)} %copy-done.7, f32[256,1024]{1,0:T(8,128)S(1)} %reshape.132, f32[32,8,8,128]{3,2,1,0:T(8,128)S(1)} %bitcast.112, f32[1024]{0:T(1024)S(1)} %broadcast_bitcast_fusion), kind=kOutput, calls=%fused_computation.15 | convolution fusion | flops 1076625408 | bytes 7868416 | tf_op jit(solution)/shard_map/dot_general | solution.py:139
  317.7 34.4 %reduce-scatter.2.cloned.1.call-done = bf16[64,2048]{1,0:T(8,128)(2,1)} async-done(((bf16[256,2048]{1,0:T(8,128)(2,1)}), bf16[64,2048]{1,0:T(8,128)(2,1)}) %reduce-scatter.2.cloned.1.call-update) | async-done | bytes 262160 | tf_op jit(solution)/shard_map/reduce_scatter | solution.py:138
  (73 shorter events, 14.1 us)
Async XLA Ops:
  6.5 345.6 %reduce-scatter.2.cloned.1.call-start = ((), (), s32[]{:S(2)}) async-start(), calls=%async_computation.1 | async-start | bytes 1310720 | tf_op jit(solution)/shard_map/reduce_scatter | solution.py:138
  7.3 177.9 %collective-permute-start.3 = (bf16[3,1024]{1,0:T(4,128)(2,1)S(1)}, bf16[3,1024]{1,0:T(4,128)(2,1)S(1)}, u32[]{:S(2)}, u32[]{:S(2)}) collective-permute-start(bf16[3,1024]{1,0:T(4,128)(2,1)S(1)} %slice.113), channel_id=1, source_target_pairs={{0,4},{4,8},{8,12},{12,16},{16,20},{20,24},{24,28},{1,5},{5,9},{9,... | collective-permute-start | bytes 18440 | tf_op jit(solution)/shard_map/ppermute | solution.py:18
  9.3 11.0 %collective-permute-start.2 = (bf16[3,512]{1,0:T(4,128)(2,1)S(1)}, bf16[3,512]{1,0:T(4,128)(2,1)S(1)}, u32[]{:S(2)}, u32[]{:S(2)}) collective-permute-start(bf16[3,512]{1,0:T(4,128)(2,1)S(1)} %slice.104), channel_id=1, source_target_pairs={{0,4},{4,8},{8,12},{12,16},{16,20},{20,24},{24,28},{1,5},{5,9},{9,... | collective-permute-start | bytes 9224 | tf_op jit(solution)/shard_map/ppermute | solution.py:18
  11.2 12.7 %collective-permute-start.1 = (bf16[3,512]{1,0:T(4,128)(2,1)S(1)}, bf16[3,512]{1,0:T(4,128)(2,1)S(1)}, u32[]{:S(2)}, u32[]{:S(2)}) collective-permute-start(bf16[3,512]{1,0:T(4,128)(2,1)S(1)} %slice.95), channel_id=1, source_target_pairs={{0,4},{4,8},{8,12},{12,16},{16,20},{20,24},{24,28},{1,5},{5,9},{9,... | collective-permute-start | bytes 9224 | tf_op jit(solution)/shard_map/ppermute | solution.py:18
  22.0 1.9 copy-start.6
  188.8 2.0 copy-start.4
  192.9 6.5 %copy-start = (f32[4,2,2,128,256]{4,3,2,1,0:T(8,128)}, f32[4,2,2,128,256]{4,3,2,1,0:T(8,128)S(1)}, u32[]{:S(2)}) copy-start(f32[4,2,2,128,256]{4,3,2,1,0:T(8,128)S(1)} %fusion.11) | copy-start | bytes 6291460
  201.7 1.7 copy-start.1
  204.2 1.7 copy-start.1
  206.6 3.2 copy-start.3
  209.8 1.2 copy-start.2
  209.8 1.5 copy-start.5
  214.9 16.6 %collective-permute-start = (f32[4,2,128,128]{3,2,1,0:T(8,128)S(1)}, f32[4,2,128,128]{3,2,1,0:T(8,128)S(1)}, u32[]{:S(2)}, u32[]{:S(2)}) collective-permute-start(f32[4,2,128,128]{3,2,1,0:T(8,128)S(1)} %convolution_add_fusion.6), channel_id=1, source_target_pairs={{0,4},{4,8},{8,12},{12,16},{16,20},{20,24},{24,28},{1,5},{5,9},{9,... | collective-permute-start | bytes 1572872 | tf_op jit(solution)/shard_map/while/body/eval_jaxpr/ppermute | solution.py:18
  232.1 14.3 %collective-permute-start = (f32[4,2,128,128]{3,2,1,0:T(8,128)S(1)}, f32[4,2,128,128]{3,2,1,0:T(8,128)S(1)}, u32[]{:S(2)}, u32[]{:S(2)}) collective-permute-start(f32[4,2,128,128]{3,2,1,0:T(8,128)S(1)} %convolution_add_fusion.6), channel_id=1, source_target_pairs={{0,4},{4,8},{8,12},{12,16},{16,20},{20,24},{24,28},{1,5},{5,9},{9,... | collective-permute-start | bytes 1572872 | tf_op jit(solution)/shard_map/while/body/eval_jaxpr/ppermute | solution.py:18
  247.1 13.4 %collective-permute-start = (f32[4,2,128,128]{3,2,1,0:T(8,128)S(1)}, f32[4,2,128,128]{3,2,1,0:T(8,128)S(1)}, u32[]{:S(2)}, u32[]{:S(2)}) collective-permute-start(f32[4,2,128,128]{3,2,1,0:T(8,128)S(1)} %convolution_add_fusion.6), channel_id=1, source_target_pairs={{0,4},{4,8},{8,12},{12,16},{16,20},{20,24},{24,28},{1,5},{5,9},{9,... | collective-permute-start | bytes 1572872 | tf_op jit(solution)/shard_map/while/body/eval_jaxpr/ppermute | solution.py:18
  261.1 12.5 %collective-permute-start = (f32[4,2,128,128]{3,2,1,0:T(8,128)S(1)}, f32[4,2,128,128]{3,2,1,0:T(8,128)S(1)}, u32[]{:S(2)}, u32[]{:S(2)}) collective-permute-start(f32[4,2,128,128]{3,2,1,0:T(8,128)S(1)} %convolution_add_fusion.6), channel_id=1, source_target_pairs={{0,4},{4,8},{8,12},{12,16},{16,20},{20,24},{24,28},{1,5},{5,9},{9,... | collective-permute-start | bytes 1572872 | tf_op jit(solution)/shard_map/while/body/eval_jaxpr/ppermute | solution.py:18
  274.3 11.6 %collective-permute-start = (f32[4,2,128,128]{3,2,1,0:T(8,128)S(1)}, f32[4,2,128,128]{3,2,1,0:T(8,128)S(1)}, u32[]{:S(2)}, u32[]{:S(2)}) collective-permute-start(f32[4,2,128,128]{3,2,1,0:T(8,128)S(1)} %convolution_add_fusion.6), channel_id=1, source_target_pairs={{0,4},{4,8},{8,12},{12,16},{16,20},{20,24},{24,28},{1,5},{5,9},{9,... | collective-permute-start | bytes 1572872 | tf_op jit(solution)/shard_map/while/body/eval_jaxpr/ppermute | solution.py:18
  286.5 10.5 %collective-permute-start = (f32[4,2,128,128]{3,2,1,0:T(8,128)S(1)}, f32[4,2,128,128]{3,2,1,0:T(8,128)S(1)}, u32[]{:S(2)}, u32[]{:S(2)}) collective-permute-start(f32[4,2,128,128]{3,2,1,0:T(8,128)S(1)} %convolution_add_fusion.6), channel_id=1, source_target_pairs={{0,4},{4,8},{8,12},{12,16},{16,20},{20,24},{24,28},{1,5},{5,9},{9,... | collective-permute-start | bytes 1572872 | tf_op jit(solution)/shard_map/while/body/eval_jaxpr/ppermute | solution.py:18
  297.7 10.8 %collective-permute-start = (f32[4,2,128,128]{3,2,1,0:T(8,128)S(1)}, f32[4,2,128,128]{3,2,1,0:T(8,128)S(1)}, u32[]{:S(2)}, u32[]{:S(2)}) collective-permute-start(f32[4,2,128,128]{3,2,1,0:T(8,128)S(1)} %convolution_add_fusion.6), channel_id=1, source_target_pairs={{0,4},{4,8},{8,12},{12,16},{16,20},{20,24},{24,28},{1,5},{5,9},{9,... | collective-permute-start | bytes 1572872 | tf_op jit(solution)/shard_map/while/body/eval_jaxpr/ppermute | solution.py:18
  311.7 1.4 copy-start.7
Sparse Core Ops, SparseCore 0:
  317.8 34.2 reduce-scatter.1
where the time goes:
time: 362 us; the launch traced here: 359 us
  other arithmetic  170 us (47%)
  waiting for transfers between devices  115 us (32%)
  matrix products  34.3 us (9%)
  between operations  13.8 us (4%)
  starting transfers between devices  12.9 us (4%)
  local copies, waits for them, and re-layouts  12.5 us (3%)
    another operation x4, other arithmetic, shards(): lax.linalg.triangular_solve(system, right_side, left_side=True, lower=Tru...  158 us
    ppermute x10, waiting for transfers between devices, shifted(): return lax.ppermute(array, axis, pairs)  80.6 us
    reduce_scatter x1, waiting for transfers between devices, shards(): lax.psum_scatter(jnp.dot(hidden, out_weight, preferred_element_type=jnp.f...  34.4 us
    ppermute x10, starting transfers between devices, shifted(): return lax.ppermute(array, axis, pairs)  12.9 us
  transfers between devices with their start and end apart: 11, of which 8 were waited for; matrix products, arithmetic and copies ran while one was open for 48% of the time, Pallas kernels for 0%

commit v1 on v0

v1 whole, which is shorter than its diff:
```python
import functools

import jax
import jax.numpy as jnp
from jax import lax
from jax.experimental import pallas as pl
from jax.experimental.pallas import tpu as pltpu
from jax.sharding import PartitionSpec as P

DK = 128
HALF = 128
RIM = 16
EPSILON = 1e-06
MESH = pl.DeviceIdType.MESH
f32 = jnp.float32
bf16 = jnp.bfloat16
STATE = f32
CHUNK = 512


def dot(a, b):
    return jnp.dot(a.astype(bf16), b.astype(bf16), preferred_element_type=f32)


def dot_nt(a, b, precision=None):
    return lax.dot_general(
        a, b, (((1,), (1,)), ((), ())), precision=precision, preferred_element_type=f32
    )


def dot_tn(a, b):
    return lax.dot_general(
        a.astype(bf16), b.astype(bf16), (((0,), (0,)), ((), ())), preferred_element_type=f32
    )


def silu(x):
    return x / (1.0 + jnp.exp(-x))


def lower_inverses(systems, masks_ref):
    size = systems[0].shape[0]
    row = lax.broadcasted_iota(jnp.int32, (size, size), 0)
    col = lax.broadcasted_iota(jnp.int32, (size, size), 1)
    eye = (row == col).astype(f32)
    lows = [low.astype(bf16) for low in systems]
    inverses = [eye - (low * masks_ref[0]).astype(f32) for low in lows]
    for level in range(1, masks_ref.shape[0]):
        held = [inverse.astype(bf16) for inverse in inverses]
        inner = [dot(low * masks_ref[level], x) for low, x in zip(lows, held)]
        inverses = [old - dot(x, y) for old, x, y in zip(inverses, held, inner)]
    return inverses


def kernel(
    seq_count,
    head_count,
    q_ref,
    k_ref,
    v_ref,
    g_ref,
    beta_ref,
    decay_ref,
    cq_ref,
    ck_ref,
    cv_ref,
    gain_ref,
    w_hbm,
    out_ref,
    rim_q,
    rim_k,
    rim_v,
    conv_s,
    masks_s,
    ccol_s,
    bcol_s,
    crow_s,
    inject_s,
    transit_s,
    end_s,
    local_s,
    couple_s,
    send_s,
    recv_s,
    hidden_s,
    w_s,
    part_s,
    gather_s,
    w_sem,
    rim_send,
    rim_recv,
    state_send,
    state_recv,
    part_send,
    part_recv,
):
    me = lax.axis_index("seq")
    mine = lax.axis_index("head")
    length, key_cols = q_ref.shape
    key_heads = key_cols // DK
    value_heads = v_ref.shape[1] // DK
    ratio = value_heads // key_heads
    has_before = me > 0
    has_after = me < seq_count - 1
    after = lax.rem(me + 1, seq_count)
    before = lax.rem(me + seq_count - 1, seq_count)

    w_copy = pltpu.make_async_copy(w_hbm, w_s, w_sem)
    w_copy.start()

    barrier = pltpu.get_barrier_semaphore()

    @pl.when(has_before)
    def _():
        pl.semaphore_signal(barrier, inc=1, device_id={"seq": before}, device_id_type=MESH)

    @pl.when(has_after)
    def _():
        pl.semaphore_signal(barrier, inc=1, device_id={"seq": after}, device_id_type=MESH)

    for step in range(1, head_count):
        pl.semaphore_signal(
            barrier,
            inc=1,
            device_id={"head": lax.rem(mine + step, head_count)},
            device_id_type=MESH,
        )
    pl.semaphore_wait(
        barrier, head_count - 1 + has_before.astype(jnp.int32) + has_after.astype(jnp.int32)
    )

    def rim_copies():
        return [
            pltpu.make_async_remote_copy(
                src_ref=source.at[pl.ds(length - RIM, RIM)],
                dst_ref=target,
                send_sem=rim_send.at[slot],
                recv_sem=rim_recv.at[slot],
                device_id={"seq": after},
                device_id_type=MESH,
            )
            for slot, (source, target) in enumerate(
                ((q_ref, rim_q), (k_ref, rim_k), (v_ref, rim_v))
            )
        ]

    @pl.when(has_after)
    def _():
        for copy in rim_copies():
            copy.start()

    @pl.when(jnp.logical_not(has_before))
    def _():
        rim_q[...] = jnp.zeros_like(rim_q)
        rim_k[...] = jnp.zeros_like(rim_k)
        rim_v[...] = jnp.zeros_like(rim_v)
        recv_s[...] = jnp.zeros_like(recv_s)

    row = lax.broadcasted_iota(jnp.int32, (HALF, HALF), 0)
    col = lax.broadcasted_iota(jnp.int32, (HALF, HALF), 1)
    for level in range(masks_s.shape[0]):
        wide = ((row >> (level + 1)) == (col >> (level + 1))) & (
            ((row >> level) & 1) == 1
        ) & (((col >> level) & 1) == 0)
        masks_s[level] = wide.astype(f32).astype(bf16)
    inclusive = row >= col
    strictly = row > col

    long_row = lax.broadcasted_iota(jnp.int32, (length, length), 0)
    long_col = lax.broadcasted_iota(jnp.int32, (length, length), 1)
    tril = (long_row >= long_col).astype(f32)
    eye = (long_row == long_col).astype(f32)
    highest = lax.Precision.HIGHEST
    decay_all = decay_ref[...]
    sums_row = dot_nt(decay_all, tril, highest)
    sums_col = dot_nt(tril, decay_all, highest)
    beta_col = dot_nt(eye, beta_ref[...], highest)
    for head in range(value_heads):
        ccol_s[head] = jnp.broadcast_to(sums_col[:, head : head + 1], (length, DK))
        bcol_s[head] = jnp.broadcast_to(beta_col[:, head : head + 1], (length, DK))
        crow_s[head] = jnp.broadcast_to(sums_row[head : head + 1, :], (8, length))

    @pl.when(has_before)
    def _():
        for copy in rim_copies():
            copy.wait_recv()

    def conv(ref, rim, taps_ref, columns, slot):
        conv_s[slot, 0:RIM, :] = rim[:, columns].astype(f32)
        conv_s[slot, RIM : RIM + length, :] = ref[:, columns].astype(f32)
        taps = taps_ref[:, columns].astype(f32)
        count = taps.shape[0]
        total = None
        for offset in range(count):
            first = RIM - count + 1 + offset
            term = taps[offset : offset + 1, :] * conv_s[slot, first : first + length, :]
            total = term if total is None else total + term
        return silu(total)

    def local(group, carry):
        columns = pl.ds(pl.multiple_of(group * DK, DK), DK)
        q = conv(q_ref, rim_q, cq_ref, columns, 0)
        k = conv(k_ref, rim_k, ck_ref, columns, 1)
        k = k * lax.rsqrt(jnp.sum(k * k, axis=-1, keepdims=True) + EPSILON)
        kb = k.astype(bf16)
        kk = dot_nt(kb, kb)
        qk = dot_nt(q.astype(bf16), kb)
        zero = jnp.zeros((HALF, HALF), f32)
        states = []
        systems = []
        for r in range(ratio):
            head = group * ratio + r
            v_columns = pl.ds(pl.multiple_of(head * DK, DK), DK)
            v = conv(v_ref, rim_v, cv_ref, v_columns, 2 + r)
            c = ccol_s[head]
            b = bcol_s[head]
            along = crow_s[head][0:1, :]
            d11 = jnp.exp(jnp.where(inclusive, c[:HALF] - along[:, :HALF], -1e30))
            d22 = jnp.exp(jnp.where(inclusive, c[HALF:] - along[:, HALF:], -1e30))
            d21 = jnp.exp(c[HALF:] - along[:, :HALF])
            l11 = jnp.where(strictly, b[:HALF] * d11 * kk[:HALF, :HALF], 0.0)
            l22 = jnp.where(strictly, b[HALF:] * d22 * kk[HALF:, HALF:], 0.0)
            l21 = b[HALF:] * d21 * kk[HALF:, :HALF]
            systems += [l11, l22]
            states.append((head, v, c, b, d11, d22, d21, l21))
        inverses = lower_inverses(systems, masks_s)
        for r in range(ratio):
            head, v, c, b, d11, d22, d21, l21 = states[r]
            x11, x22 = inverses[2 * r], inverses[2 * r + 1]
            x21 = -dot(x22, dot(l21, x11))
            inverse = jnp.concatenate(
                [jnp.concatenate([x11, zero], axis=1), jnp.concatenate([x21, x22], axis=1)], axis=0
            )
            e = jnp.exp(c)
            right = jnp.concatenate([b * v, b * e * k], axis=1)
            solved = dot(inverse, right).astype(bf16)
            attention = jnp.concatenate(
                [
                    jnp.concatenate([d11 * qk[:HALF, :HALF], zero], axis=1),
                    jnp.concatenate([d21 * qk[HALF:, :HALF], d22 * qk[HALF:, HALF:]], axis=1),
                ],
                axis=0,
            )
            seen = dot(attention, solved)
            local_s[head] = seen[:, :DK]
            couple_s[head] = (e * q - seen[:, DK:]).astype(bf16)
            last = c[length - 1 : length, :]
            moved = dot_tn(jnp.exp(last - c) * k, solved)
            inject_s[head] = moved[:, :DK]
            transit_s[head] = moved[:, DK:].astype(bf16)
            end_s[head] = jnp.broadcast_to(jnp.exp(last), (8, DK))
        return carry

    lax.fori_loop(0, key_heads, local, 0)

    def state_copy(head):
        return pltpu.make_async_remote_copy(
            src_ref=send_s.at[head],
            dst_ref=recv_s.at[head],
            send_sem=state_send.at[head],
            recv_sem=state_recv.at[head],
            device_id={"seq": after},
            device_id_type=MESH,
        )

    gain = gain_ref[...].astype(f32)

    def relay(head, carry):
        @pl.when(has_before)
        def _():
            state_copy(head).wait_recv()

        state = recv_s[head].astype(f32)
        held = state.astype(bf16)

        @pl.when(has_after)
        def _():
            following = (
                end_s[head][0:1, :] * state + inject_s[head] - dot(transit_s[head], held)
            )
            send_s[head] = following.astype(STATE)
            state_copy(head).start()

        core = local_s[head] + dot(couple_s[head], held)
        scale = lax.rsqrt(jnp.mean(core * core, axis=-1, keepdims=True) + EPSILON)
        columns = pl.ds(pl.multiple_of(head * DK, DK), DK)
        gate = g_ref[:, columns].astype(f32)
        hidden_s[:, columns] = (core * scale * gain * silu(gate)).astype(bf16)
        return carry

    lax.fori_loop(0, value_heads, relay, 0)
    w_copy.wait()

    chunks, _, rows, width = part_s.shape

    def part_copy(chunk, step):
        target = lax.rem(mine + step, head_count)
        return pltpu.make_async_remote_copy(
            src_ref=part_s.at[chunk, target],
            dst_ref=gather_s.at[chunk, step - 1],
            send_sem=part_send.at[chunk, step - 1],
            recv_sem=part_recv.at[chunk, step - 1],
            device_id={"head": target},
            device_id_type=MESH,
        )

    for chunk in range(chunks):
        product = jnp.dot(
            hidden_s[...],
            w_s[:, chunk * width : (chunk + 1) * width],
            preferred_element_type=f32,
        ).astype(bf16)
        for target in range(head_count):
            part_s[chunk, target] = product[target * rows : (target + 1) * rows]
        for step in range(1, head_count):
            part_copy(chunk, step).start()
    for chunk in range(chunks):
        total = part_s[chunk, mine].astype(f32)
        for step in range(1, head_count):
            part_copy(chunk, step).wait_recv()
            total = total + gather_s[chunk, step - 1].astype(f32)
        out_ref[:, chunk * width : (chunk + 1) * width] = total.astype(bf16)

    for chunk in range(chunks):
        for step in range(1, head_count):
            part_copy(chunk, step).wait_send()

    @pl.when(has_after)
    def _():
        for copy in rim_copies():
            copy.wait_send()
        for head in range(value_heads):
            state_copy(head).wait_send()


def shards(seq_count, head_count, *arrays):
    query_proj, key_proj, value_proj, gate_proj, strength, log_decay = arrays[:6]
    conv_query, conv_key, conv_value, norm_gain, out_weight = arrays[6:]
    length, key_cols = query_proj.shape
    value_cols = value_proj.shape[1]
    heads = value_cols // DK
    ratio = value_cols // key_cols
    width = out_weight.shape[1]
    rows = length // head_count
    chunks = width // CHUNK
    vmem = pl.BlockSpec(memory_space=pltpu.VMEM)
    others = head_count - 1
    return pl.pallas_call(
        functools.partial(kernel, seq_count, head_count),
        out_shape=jax.ShapeDtypeStruct((rows, width), bf16),
        in_specs=[vmem] * 10 + [pl.BlockSpec(memory_space=pl.ANY)],
        out_specs=vmem,
        scratch_shapes=[
            pltpu.VMEM((RIM, key_cols), bf16),
            pltpu.VMEM((RIM, key_cols), bf16),
            pltpu.VMEM((RIM, value_cols), bf16),
            pltpu.VMEM((2 + ratio, RIM + length, DK), f32),
            pltpu.VMEM((7, HALF, HALF), bf16),
            pltpu.VMEM((heads, length, DK), f32),
            pltpu.VMEM((heads, length, DK), f32),
            pltpu.VMEM((heads, 8, length), f32),
            pltpu.VMEM((heads, DK, DK), f32),
            pltpu.VMEM((heads, DK, DK), bf16),
            pltpu.VMEM((heads, 8, DK), f32),
            pltpu.VMEM((heads, length, DK), f32),
            pltpu.VMEM((heads, length, DK), bf16),
            pltpu.VMEM((heads, DK, DK), STATE),
            pltpu.VMEM((heads, DK, DK), STATE),
            pltpu.VMEM((length, value_cols), bf16),
            pltpu.VMEM((value_cols, width), bf16),
            pltpu.VMEM((chunks, head_count, rows, CHUNK), bf16),
            pltpu.VMEM((chunks, others, rows, CHUNK), bf16),
            pltpu.SemaphoreType.DMA,
            pltpu.SemaphoreType.DMA((3,)),
            pltpu.SemaphoreType.DMA((3,)),
            pltpu.SemaphoreType.DMA((heads,)),
            pltpu.SemaphoreType.DMA((heads,)),
            pltpu.SemaphoreType.DMA((chunks, others)),
            pltpu.SemaphoreType.DMA((chunks, others)),
        ],
        compiler_params=pltpu.CompilerParams(
            collective_id=0, has_side_effects=True, vmem_limit_bytes=48 * 1024 * 1024
        ),
    )(
        query_proj,
        key_proj,
        value_proj,
        gate_proj,
        strength,
        log_decay,
        conv_query,
        conv_key,
        conv_value,
        norm_gain.reshape(1, DK),
        out_weight,
    )


def solution(mesh):
    placed = (
        P("seq", "head"),
        P("seq", "head"),
        P("seq", "head"),
        P("seq", "head"),
        P("head", "seq"),
        P("head", "seq"),
        P(None, "head"),
        P(None, "head"),
        P(None, "head"),
        P(),
        P("head", None),
    )
    body = functools.partial(shards, mesh.shape["seq"], mesh.shape["head"])
    return jax.shard_map(
        body, mesh=mesh, in_specs=placed, out_specs=P(("seq", "head"), None), check_vma=False
    )
```

time: 362 us -> 71.1 us (0.20)
  other arithmetic: 170 us -> 0 us
  waiting for transfers between devices: 115 us -> 0 us
  Pallas kernels: 0 us -> 59.6 us
  matrix products: 34.3 us -> 0 us
  between operations: 13.8 us -> 0.02 us
  starting transfers between devices: 12.9 us -> 0 us
    another operation x7 -> x0, other arithmetic: 161 us -> none  [the longest x4 158 us: shards(): lax.linalg.triangular_solve(system, right_side, left_side=True, lower=Tru...]
    ppermute x10 -> x0, waiting for transfers between devices: 80.6 us -> none  [shifted(): return lax.ppermute(array, axis, pairs)]
    pallas_call x0 -> x1, Pallas kernels: none -> 59.6 us  [shards(): pl.pallas_call(functools.partial(kernel, seq_count, head_count), out_shap...]
    reduce_scatter x1 -> x0, waiting for transfers between devices: 34.4 us -> none  [shards(): lax.psum_scatter(jnp.dot(hidden, out_weight, preferred_element_type=jnp.f...]
    dot_general x21 -> x0, matrix products: 32.3 us -> none  [the longest x11 7.1 us: apply_map(): return jnp.einsum('hrke,hrev->hrkv', matrix, state_now, precision=highest)]
    ppermute x10 -> x0, starting transfers between devices: 12.9 us -> none  [shifted(): return lax.ppermute(array, axis, pairs)]
    unnamed x16 -> x23, local copies, waits for them, and re-layouts: 0.47 us -> 11 us
    slice x7 -> x0, local copies, waits for them, and re-layouts: 4.76 us -> none  [the longest x3 2.55 us: conv_silu(): summed = summed + conv_taps[offset] * padded[offset:offset + length]]
  transfers between devices with their start and end apart: 11 -> 0, of which waited for: 8 -> 0; matrix products, arithmetic and copies ran while one was open for 48% -> 0% of each run, Pallas kernels for 0% -> 0%
where the time goes in v1:
time: 71.1 us; the launch traced here: 70.6 us
  Pallas kernels  59.6 us (84%)
  local copies, waits for them, and re-layouts  11 us (15%)
    pallas_call x1, Pallas kernels, shards(): pl.pallas_call(functools.partial(kernel, seq_count, head_count), out_shap...  59.6 us
    unnamed x23, local copies, waits for them, and re-layouts  11 us

profile of v1, /device:TPU:29, one launch (start us, length us, event | category | flops | bytes accessed | tf_op | source)
XLA Modules:
  0.0 70.6 jit_solution(13152666021283577143)
XLA Ops:
  0.0 0.0 copy-start
  0.0 2.2 %copy-done = bf16[1024,2048]{1,0:T(8,128)(2,1)S(1)} copy-done((bf16[1024,2048]{1,0:T(8,128)(2,1)S(1)}, bf16[1024,2048]{1,0:T(8,128)(2,1)}, u32[]{:S(2)}) %copy-start) | copy-done | bytes 4194328
  2.2 0.0 copy-start.1
  2.2 1.0 %copy-done.1 = bf16[256,1024]{1,0:T(8,128)(2,1)S(1)} copy-done((bf16[256,1024]{1,0:T(8,128)(2,1)S(1)}, bf16[256,1024]{1,0:T(8,128)(2,1)}, u32[]{:S(2)}) %copy-start.1) | copy-done | bytes 524312
  3.2 0.0 copy-start.2
  3.2 1.0 %copy-done.2 = bf16[256,1024]{1,0:T(8,128)(2,1)S(1)} copy-done((bf16[256,1024]{1,0:T(8,128)(2,1)S(1)}, bf16[256,1024]{1,0:T(8,128)(2,1)}, u32[]{:S(2)}) %copy-start.2) | copy-done | bytes 524312
  4.3 0.0 copy-start.3
  4.3 0.9 %copy-done.3 = bf16[256,512]{1,0:T(8,128)(2,1)S(1)} copy-done((bf16[256,512]{1,0:T(8,128)(2,1)S(1)}, bf16[256,512]{1,0:T(8,128)(2,1)}, u32[]{:S(2)}) %copy-start.3) | copy-done | bytes 262168
  5.2 0.0 copy-start.4
  5.2 0.9 %copy-done.4 = bf16[256,512]{1,0:T(8,128)(2,1)S(1)} copy-done((bf16[256,512]{1,0:T(8,128)(2,1)S(1)}, bf16[256,512]{1,0:T(8,128)(2,1)}, u32[]{:S(2)}) %copy-start.4) | copy-done | bytes 262168
  6.2 0.0 copy-start.5
  6.2 0.7 copy-done.5
  6.9 0.0 copy-start.6
  6.9 0.7 copy-done.6
  7.6 0.0 copy-start.7
  7.6 0.7 copy-done.7
  8.3 0.0 copy-start.8
  8.3 0.7 copy-done.8
  9.0 0.0 copy-start.9
  9.0 0.7 copy-done.9
  9.6 0.0 copy-start.10
  9.6 0.7 copy-done.10
  10.3 59.6 %shard_map.109 = bf16[64,2048]{1,0:T(8,128)(2,1)S(1)} custom-call(bf16[256,512]{1,0:T(8,128)(2,1)S(1)} %copy-done.3, bf16[256,512]{1,0:T(8,128)(2,1)S(1)} %copy-done.4, bf16[256,1024]{1,0:T(8,128)(2,1)S(1)} %copy-done.1, bf16[256,1024]{1,0:T(8,128)(2,1)S(1)} %copy-done.2, f32[8,256]{1,0:T(8,128)S(1)} %copy-done.5, f32[8,256]{1,0:T(8,128)S(1)} %copy-done.6, ...), custom_call_target="tpu_custom_call" | custom-call | tf_op jit(solution)/shard_map/pallas_call | solution.py:348
  69.9 0.7 copy.13
Async XLA Ops:
  0.0 2.2 %copy-start = (bf16[1024,2048]{1,0:T(8,128)(2,1)S(1)}, bf16[1024,2048]{1,0:T(8,128)(2,1)}, u32[]{:S(2)}) copy-start(bf16[1024,2048]{1,0:T(8,128)(2,1)} %w_hbm.1) | copy-start | bytes 12582916
  2.2 1.0 %copy-start.1 = (bf16[256,1024]{1,0:T(8,128)(2,1)S(1)}, bf16[256,1024]{1,0:T(8,128)(2,1)}, u32[]{:S(2)}) copy-start(bf16[256,1024]{1,0:T(8,128)(2,1)} %v_ref.1) | copy-start | bytes 1572868
  3.2 1.0 %copy-start.2 = (bf16[256,1024]{1,0:T(8,128)(2,1)S(1)}, bf16[256,1024]{1,0:T(8,128)(2,1)}, u32[]{:S(2)}) copy-start(bf16[256,1024]{1,0:T(8,128)(2,1)} %g_ref.1) | copy-start | bytes 1572868
  4.3 0.9 %copy-start.3 = (bf16[256,512]{1,0:T(8,128)(2,1)S(1)}, bf16[256,512]{1,0:T(8,128)(2,1)}, u32[]{:S(2)}) copy-start(bf16[256,512]{1,0:T(8,128)(2,1)} %q_ref.1) | copy-start | bytes 786436
  5.2 0.9 %copy-start.4 = (bf16[256,512]{1,0:T(8,128)(2,1)S(1)}, bf16[256,512]{1,0:T(8,128)(2,1)}, u32[]{:S(2)}) copy-start(bf16[256,512]{1,0:T(8,128)(2,1)} %k_ref.1) | copy-start | bytes 786436
  6.2 0.7 copy-start.5
  6.9 0.7 copy-start.6
  7.6 0.7 copy-start.7
  8.3 0.7 copy-start.8
  9.0 0.7 copy-start.9
  9.6 0.7 copy-start.10

commit v2 on v1

v2 whole, which is shorter than its diff:
```python
import functools

import jax
import jax.numpy as jnp
from jax import lax
from jax.experimental import pallas as pl
from jax.experimental.pallas import tpu as pltpu
from jax.sharding import PartitionSpec as P

DK = 128
HALF = 128
RIM = 16
EPSILON = 1e-06
MESH = pl.DeviceIdType.MESH
f32 = jnp.float32
bf16 = jnp.bfloat16
CHUNK = 512
NOTE = 16


def dot(a, b):
    return jnp.dot(a.astype(bf16), b.astype(bf16), preferred_element_type=f32)


def dot_nt(a, b, precision=None):
    return lax.dot_general(
        a, b, (((1,), (1,)), ((), ())), precision=precision, preferred_element_type=f32
    )


def dot_tn(a, b):
    return lax.dot_general(
        a.astype(bf16), b.astype(bf16), (((0,), (0,)), ((), ())), preferred_element_type=f32
    )


def silu(x):
    return x / (1.0 + jnp.exp(-x))


def lower_inverses(systems, masks_ref):
    size = systems[0].shape[0]
    row = lax.broadcasted_iota(jnp.int32, (size, size), 0)
    col = lax.broadcasted_iota(jnp.int32, (size, size), 1)
    eye = (row == col).astype(f32)
    lows = [low.astype(bf16) for low in systems]
    inverses = [eye - (low * masks_ref[0]).astype(f32) for low in lows]
    for level in range(1, masks_ref.shape[0]):
        held = [inverse.astype(bf16) for inverse in inverses]
        inner = [dot(low * masks_ref[level], x) for low, x in zip(lows, held)]
        inverses = [old - dot(x, y) for old, x, y in zip(inverses, held, inner)]
    return inverses


def kernel(
    seq_count,
    head_count,
    q_hbm,
    k_hbm,
    v_hbm,
    g_hbm,
    beta_hbm,
    decay_hbm,
    cq_hbm,
    ck_hbm,
    cv_hbm,
    gain_hbm,
    w_hbm,
    out_ref,
    q_ref,
    k_ref,
    v_ref,
    g_ref,
    beta_ref,
    decay_ref,
    cq_ref,
    ck_ref,
    cv_ref,
    gain_ref,
    w_s,
    rim_q,
    rim_k,
    rim_v,
    conv_s,
    masks_s,
    ccol_s,
    bcol_s,
    crow_s,
    pair_s,
    inject_s,
    transit_s,
    end_s,
    local_s,
    couple_s,
    send_s,
    recv_s,
    hidden_s,
    part_s,
    near_s,
    sum_s,
    gather_s,
    load_sem,
    rim_send,
    rim_recv,
    pair_send,
    pair_recv,
    state_send,
    state_recv,
    near_send,
    near_recv,
    far_send,
    far_recv,
):
    me = lax.axis_index("seq")
    mine = lax.axis_index("head")
    length, key_cols = q_ref.shape
    key_heads = key_cols // DK
    value_heads = v_ref.shape[1] // DK
    ratio = value_heads // key_heads
    stages = seq_count // 2
    stage = lax.div(me, 2)
    parity = lax.rem(me, 2)
    columns_x = head_count // 2
    core = lax.rem(mine, 2)
    across = lax.div(mine, 2)
    has_before = me > 0
    has_after = me < seq_count - 1
    has_earlier = stage > 0
    has_later = stage < stages - 1
    after = lax.rem(me + 1, seq_count)
    before = lax.rem(me + seq_count - 1, seq_count)
    later = lax.rem(me + 2, seq_count)
    earlier = lax.rem(me + seq_count - 2, seq_count)
    partner = stage * 2 + 1 - parity
    twin = across * 2 + 1 - core

    def at_seq(index):
        return dict(device_id={"seq": index}, device_id_type=MESH)

    def at_head(index):
        return dict(device_id={"head": index}, device_id_type=MESH)

    loads = [
        pltpu.make_async_copy(source, target, load_sem.at[slot])
        for slot, (source, target) in enumerate(
            (
                (decay_hbm, decay_ref),
                (beta_hbm, beta_ref),
                (q_hbm, q_ref),
                (k_hbm, k_ref),
                (v_hbm, v_ref),
                (cq_hbm, cq_ref),
                (ck_hbm, ck_ref),
                (cv_hbm, cv_ref),
                (gain_hbm, gain_ref),
                (g_hbm, g_ref),
                (w_hbm, w_s),
            )
        )
    ]
    for load in loads:
        load.start()

    barrier = pltpu.get_barrier_semaphore()
    for there, index in (
        (has_before, before),
        (has_after, after),
        (has_earlier, earlier),
        (has_later, later),
    ):

        @pl.when(there)
        def _(index=index):
            pl.semaphore_signal(barrier, inc=1, **at_seq(index))

    pl.semaphore_signal(barrier, inc=1, **at_head(twin))
    for step in range(1, columns_x):
        other = lax.rem(across + step, columns_x) * 2 + core
        pl.semaphore_signal(barrier, inc=1, **at_head(other))
    greeted = columns_x
    for there in (has_before, has_after, has_earlier, has_later):
        greeted = greeted + there.astype(jnp.int32)
    pl.semaphore_wait(barrier, greeted)

    def rim_copies():
        return [
            pltpu.make_async_remote_copy(
                src_ref=source.at[pl.ds(length - RIM, RIM)],
                dst_ref=target,
                send_sem=rim_send.at[slot],
                recv_sem=rim_recv.at[slot],
                **at_seq(after),
            )
            for slot, (source, target) in enumerate(
                ((q_hbm, rim_q), (k_hbm, rim_k), (v_hbm, rim_v))
            )
        ]

    @pl.when(has_after)
    def _():
        for copy in rim_copies():
            copy.start()

    @pl.when(jnp.logical_not(has_before))
    def _():
        rim_q[...] = jnp.zeros_like(rim_q)
        rim_k[...] = jnp.zeros_like(rim_k)
        rim_v[...] = jnp.zeros_like(rim_v)

    @pl.when(jnp.logical_not(has_earlier))
    def _():
        recv_s[...] = jnp.zeros_like(recv_s)

    row = lax.broadcasted_iota(jnp.int32, (HALF, HALF), 0)
    col = lax.broadcasted_iota(jnp.int32, (HALF, HALF), 1)
    for level in range(masks_s.shape[0]):
        wide = ((row >> (level + 1)) == (col >> (level + 1))) & (
            ((row >> level) & 1) == 1
        ) & (((col >> level) & 1) == 0)
        masks_s[level] = wide.astype(f32).astype(bf16)

    loads[0].wait()
    loads[1].wait()
    long_row = lax.broadcasted_iota(jnp.int32, (length, length), 0)
    long_col = lax.broadcasted_iota(jnp.int32, (length, length), 1)
    tril = (long_row >= long_col).astype(f32)
    eye = (long_row == long_col).astype(f32)
    highest = lax.Precision.HIGHEST
    decay_all = decay_ref[...]
    sums_row = dot_nt(decay_all, tril, highest)
    sums_col = dot_nt(tril, decay_all, highest)
    beta_col = dot_nt(eye, beta_ref[...], highest)
    for head in range(value_heads):
        ccol_s[head] = jnp.broadcast_to(sums_col[:, head : head + 1], (length, DK))
        bcol_s[head] = jnp.broadcast_to(beta_col[:, head : head + 1], (length, DK))
        crow_s[head] = jnp.broadcast_to(sums_row[head : head + 1, :], (8, length))

    for load in loads[2:10]:
        load.wait()

    @pl.when(has_before)
    def _():
        for copy in rim_copies():
            copy.wait_recv()

    gain = gain_ref[...].astype(f32)

    def conv(ref, rim, taps_ref, columns, slot):
        conv_s[slot, 0:RIM, :] = rim[:, columns].astype(f32)
        conv_s[slot, RIM : RIM + length, :] = ref[:, columns].astype(f32)
        taps = taps_ref[:, columns].astype(f32)
        count = taps.shape[0]
        total = None
        for offset in range(count):
            first = RIM - count + 1 + offset
            term = taps[offset : offset + 1, :] * conv_s[slot, first : first + length, :]
            total = term if total is None else total + term
        return silu(total)

    def pair_copy(head):
        return pltpu.make_async_remote_copy(
            src_ref=pair_s.at[parity, head],
            dst_ref=pair_s.at[parity, head],
            send_sem=pair_send.at[head],
            recv_sem=pair_recv.at[head],
            **at_seq(partner),
        )

    def state_copy(head):
        return pltpu.make_async_remote_copy(
            src_ref=send_s.at[head],
            dst_ref=recv_s.at[head],
            send_sem=state_send.at[head],
            recv_sem=state_recv.at[head],
            **at_seq(later),
        )

    def local(group):
        inclusive = row >= col
        strictly = row > col
        columns = pl.ds(pl.multiple_of(group * DK, DK), DK)
        q = conv(q_ref, rim_q, cq_ref, columns, 0)
        k = conv(k_ref, rim_k, ck_ref, columns, 1)
        k = k * lax.rsqrt(jnp.sum(k * k, axis=-1, keepdims=True) + EPSILON)
        kb = k.astype(bf16)
        kk = dot_nt(kb, kb)
        qk = dot_nt(q.astype(bf16), kb)
        zero = jnp.zeros((HALF, HALF), f32)
        states = []
        systems = []
        for r in range(ratio):
            head = group * ratio + r
            v_columns = pl.ds(pl.multiple_of(head * DK, DK), DK)
            v = conv(v_ref, rim_v, cv_ref, v_columns, 2 + r)
            c = ccol_s[head]
            b = bcol_s[head]
            along = crow_s[head][0:1, :]
            d11 = jnp.exp(jnp.where(inclusive, c[:HALF] - along[:, :HALF], -1e30))
            d22 = jnp.exp(jnp.where(inclusive, c[HALF:] - along[:, HALF:], -1e30))
            d21 = jnp.exp(c[HALF:] - along[:, :HALF])
            l11 = jnp.where(strictly, b[:HALF] * d11 * kk[:HALF, :HALF], 0.0)
            l22 = jnp.where(strictly, b[HALF:] * d22 * kk[HALF:, HALF:], 0.0)
            l21 = b[HALF:] * d21 * kk[HALF:, :HALF]
            systems += [l11, l22]
            states.append((head, v, c, b, d11, d22, d21, l21))
        inverses = lower_inverses(systems, masks_s)
        for r in range(ratio):
            head, v, c, b, d11, d22, d21, l21 = states[r]
            x11, x22 = inverses[2 * r], inverses[2 * r + 1]
            x21 = -dot(x22, dot(l21, x11))
            inverse = jnp.concatenate(
                [jnp.concatenate([x11, zero], axis=1), jnp.concatenate([x21, x22], axis=1)], axis=0
            )
            e = jnp.exp(c)
            right = jnp.concatenate([b * v, b * e * k], axis=1)
            solved = dot(inverse, right).astype(bf16)
            last = c[length - 1 : length, :]
            moved = dot_tn(jnp.exp(last - c) * k, solved)
            pair_s[parity, head, 0:DK, :] = moved[:, DK:].astype(bf16)
            pair_s[parity, head, DK : 2 * DK, :] = moved[:, :DK].astype(bf16)
            end = jnp.broadcast_to(jnp.exp(last), (NOTE, DK))
            high = end.astype(bf16)
            rest = end - high.astype(f32)
            upper = lax.broadcasted_iota(jnp.int32, (NOTE, DK), 0) < NOTE // 2
            pair_s[parity, head, 2 * DK :, :] = jnp.where(upper, high.astype(f32), rest).astype(bf16)
            pair_copy(head).start()
            attention = jnp.concatenate(
                [
                    jnp.concatenate([d11 * qk[:HALF, :HALF], zero], axis=1),
                    jnp.concatenate([d21 * qk[HALF:, :HALF], d22 * qk[HALF:, HALF:]], axis=1),
                ],
                axis=0,
            )
            seen = dot(attention, solved)
            local_s[head] = seen[:, :DK]
            couple_s[head] = (e * q - seen[:, DK:]).astype(bf16)

    def unpacked(which, head):
        note = pair_s[which, head, 2 * DK :, :].astype(f32)
        end = note[0:1, :] + note[NOTE // 2 : NOTE // 2 + 1, :]
        return end, pair_s[which, head, 0:DK, :], pair_s[which, head, DK : 2 * DK, :]

    def compose(group):
        for r in range(ratio):
            pair_copy(group * ratio + r).wait_recv()
        for r in range(ratio):
            head = group * ratio + r
            end0, map0, inject0 = unpacked(0, head)
            end1, map1, inject1 = unpacked(1, head)
            both = dot(map1, jnp.concatenate([map0, inject0], axis=1))
            transit = end1 * map0.astype(f32) + end0 * map1.astype(f32) - both[:, :DK]
            transit_s[head] = transit.astype(bf16)
            inject_s[head] = end1 * inject0.astype(f32) + inject1.astype(f32) - both[:, DK:]
            end_s[head] = jnp.broadcast_to(end1 * end0, (8, DK))

    def relay(group):
        heads = [group * ratio + r for r in range(ratio)]

        @pl.when(has_earlier)
        def _():
            for head in heads:
                state_copy(head).wait_recv()

        @pl.when(has_later)
        def _():
            for head in heads:
                held = recv_s[head]
                following = (
                    end_s[head][0:1, :] * held.astype(f32)
                    + inject_s[head]
                    - dot(transit_s[head], held)
                )
                send_s[head] = following.astype(bf16)
                state_copy(head).start()

        odd = parity == 1
        for head in heads:
            held = recv_s[head]
            end0, map0, inject0 = unpacked(0, head)
            moved = end0 * held.astype(f32) + inject0.astype(f32) - dot(map0, held)
            state = jnp.where(odd, moved, held.astype(f32)).astype(bf16)
            core_out = local_s[head] + dot(couple_s[head], state)
            scale = lax.rsqrt(jnp.mean(core_out * core_out, axis=-1, keepdims=True) + EPSILON)
            columns = pl.ds(pl.multiple_of(head * DK, DK), DK)
            gate = g_ref[:, columns].astype(f32)
            hidden_s[:, columns] = (core_out * scale * gain * silu(gate)).astype(bf16)

    def slot(turn, carry):
        @pl.when(turn < key_heads)
        def _():
            local(turn)

        @pl.when((turn >= 1) & (turn <= key_heads))
        def _():
            compose(turn - 1)

        group = turn - 1 - stage

        @pl.when((group >= 0) & (group < key_heads))
        def _():
            relay(group)

        return carry

    lax.fori_loop(0, key_heads + stages, slot, 0)
    loads[10].wait()

    chunks, _, _, rows, width = part_s.shape

    def near_copy(chunk):
        return pltpu.make_async_remote_copy(
            src_ref=part_s.at[chunk, 1 - core],
            dst_ref=near_s.at[chunk],
            send_sem=near_send.at[chunk],
            recv_sem=near_recv.at[chunk],
            **at_head(twin),
        )

    def far_copy(chunk, step):
        target = lax.rem(across + step, columns_x)
        return pltpu.make_async_remote_copy(
            src_ref=sum_s.at[chunk, target],
            dst_ref=gather_s.at[chunk, step - 1],
            send_sem=far_send.at[chunk, step - 1],
            recv_sem=far_recv.at[chunk, step - 1],
            **at_head(target * 2 + core),
        )

    def project(chunk):
        product = jnp.dot(
            hidden_s[...],
            w_s[:, chunk * width : (chunk + 1) * width],
            preferred_element_type=f32,
        ).astype(bf16)
        for target in range(head_count):
            part_s[chunk, target % 2, target // 2] = product[target * rows : (target + 1) * rows]
        near_copy(chunk).start()

    def forward(chunk):
        near_copy(chunk).wait_recv()
        sum_s[chunk] = (part_s[chunk, core].astype(f32) + near_s[chunk].astype(f32)).astype(bf16)
        for step in range(1, columns_x):
            far_copy(chunk, step).start()

    lag = 2
    for turn in range(chunks + lag):
        if turn < chunks:
            project(turn)
        if turn >= lag:
            forward(turn - lag)
    for chunk in range(chunks):
        total = part_s[chunk, core, across].astype(f32) + near_s[chunk, across].astype(f32)
        for step in range(1, columns_x):
            far_copy(chunk, step).wait_recv()
            total = total + gather_s[chunk, step - 1].astype(f32)
        out_ref[:, chunk * width : (chunk + 1) * width] = total.astype(bf16)

    for chunk in range(chunks):
        near_copy(chunk).wait_send()
        for step in range(1, columns_x):
            far_copy(chunk, step).wait_send()
    for head in range(value_heads):
        pair_copy(head).wait_send()

    @pl.when(has_after)
    def _():
        for copy in rim_copies():
            copy.wait_send()

    @pl.when(has_later)
    def _():
        for head in range(value_heads):
            state_copy(head).wait_send()


def shards(seq_count, head_count, *arrays):
    query_proj, _, value_proj = arrays[:3]
    norm_gain, out_weight = arrays[9:]
    length, key_cols = query_proj.shape
    value_cols = value_proj.shape[1]
    heads = value_cols // DK
    ratio = value_cols // key_cols
    width = out_weight.shape[1]
    rows = length // head_count
    chunks = width // CHUNK
    operands = arrays[:9] + (norm_gain.reshape(1, DK), out_weight)
    columns_x = head_count // 2
    others = max(columns_x - 1, 1)
    semaphore = pltpu.SemaphoreType.DMA
    return pl.pallas_call(
        functools.partial(kernel, seq_count, head_count),
        out_shape=jax.ShapeDtypeStruct((rows, width), bf16),
        in_specs=[pl.BlockSpec(memory_space=pltpu.HBM)] * len(operands),
        out_specs=pl.BlockSpec(memory_space=pltpu.VMEM),
        scratch_shapes=[pltpu.VMEM(array.shape, array.dtype) for array in operands]
        + [
            pltpu.VMEM((RIM, key_cols), bf16),
            pltpu.VMEM((RIM, key_cols), bf16),
            pltpu.VMEM((RIM, value_cols), bf16),
            pltpu.VMEM((2 + ratio, RIM + length, DK), f32),
            pltpu.VMEM((7, HALF, HALF), bf16),
            pltpu.VMEM((heads, length, DK), f32),
            pltpu.VMEM((heads, length, DK), f32),
            pltpu.VMEM((heads, 8, length), f32),
            pltpu.VMEM((2, heads, 2 * DK + NOTE, DK), bf16),
            pltpu.VMEM((heads, DK, DK), f32),
            pltpu.VMEM((heads, DK, DK), bf16),
            pltpu.VMEM((heads, 8, DK), f32),
            pltpu.VMEM((heads, length, DK), f32),
            pltpu.VMEM((heads, length, DK), bf16),
            pltpu.VMEM((heads, DK, DK), bf16),
            pltpu.VMEM((heads, DK, DK), bf16),
            pltpu.VMEM((length, value_cols), bf16),
            pltpu.VMEM((chunks, 2, columns_x, rows, CHUNK), bf16),
            pltpu.VMEM((chunks, columns_x, rows, CHUNK), bf16),
            pltpu.VMEM((chunks, columns_x, rows, CHUNK), bf16),
            pltpu.VMEM((chunks, others, rows, CHUNK), bf16),
            semaphore((len(operands),)),
            semaphore((3,)),
            semaphore((3,)),
            semaphore((heads,)),
            semaphore((heads,)),
            semaphore((heads,)),
            semaphore((heads,)),
            semaphore((chunks,)),
            semaphore((chunks,)),
            semaphore((chunks, others)),
            semaphore((chunks, others)),
        ],
        compiler_params=pltpu.CompilerParams(
            collective_id=0, has_side_effects=True, vmem_limit_bytes=60 * 1024 * 1024
        ),
    )(*operands)


def solution(mesh):
    placed = (
        P("seq", "head"),
        P("seq", "head"),
        P("seq", "head"),
        P("seq", "head"),
        P("head", "seq"),
        P("head", "seq"),
        P(None, "head"),
        P(None, "head"),
        P(None, "head"),
        P(),
        P("head", None),
    )
    body = functools.partial(shards, mesh.shape["seq"], mesh.shape["head"])
    return jax.shard_map(
        body, mesh=mesh, in_specs=placed, out_specs=P(("seq", "head"), None), check_vma=False
    )
```

time: 71.1 us -> 45.2 us (0.64)
  Pallas kernels: 59.6 us -> 43.4 us
  local copies, waits for them, and re-layouts: 11 us -> 1.67 us
    pallas_call x1, Pallas kernels: 59.6 us -> 43.4 us  [shards(): pl.pallas_call(functools.partial(kernel, seq_count, head_count), out_shap...]
    unnamed x23 -> x1, local copies, waits for them, and re-layouts: 11 us -> 1.67 us
where the time goes in v2:
time: 45.2 us; the launch traced here: 45.1 us
  Pallas kernels  43.4 us (96%)
  local copies, waits for them, and re-layouts  1.67 us (4%)
    pallas_call x1, Pallas kernels, shards(): pl.pallas_call(functools.partial(kernel, seq_count, head_count), out_shap...  43.4 us
    unnamed x1, local copies, waits for them, and re-layouts  1.67 us

profile of v2, /device:TPU:29, one launch (start us, length us, event | category | flops | bytes accessed | tf_op | source)
XLA Modules:
  0.0 45.1 jit_solution(7999385356599470285)
XLA Ops:
  0.0 43.4 %shard_map.109 = bf16[64,2048]{1,0:T(8,128)(2,1)} custom-call(bf16[256,512]{1,0:T(8,128)(2,1)} %q_hbm.1, bf16[256,512]{1,0:T(8,128)(2,1)} %k_hbm.1, bf16[256,1024]{1,0:T(8,128)(2,1)} %v_hbm.1, bf16[256,1024]{1,0:T(8,128)(2,1)} %g_hbm.1, f32[8,256]{1,0:T(8,128)} %beta_hbm.1, f32[8,256]{1,0:T(8,128)} %decay_hbm.1, bf16[4,512]{1,0:T(4,128)(2,1)} %cq_hbm.1, ...), custom_call_target="tpu_custom_call" | custom-call | tf_op jit(solution)/shard_map/pallas_call | solution.py:490
  43.4 1.7 %copy.13 = bf16[64,2048]{1,0:T(8,128)(2,1)} copy(bf16[64,2048]{1,0:T(8,128)(2,1)} %shard_map.109) | data formatting | bytes 524288

commit v3 on v2

--- a/solution.py
+++ b/solution.py
@@ -92,6 +92,8 @@
     end_s,
     local_s,
     couple_s,
+    attention_s,
+    solved_s,
     send_s,
     recv_s,
     hidden_s,
@@ -180,6 +182,14 @@
     greeted = columns_x
     for there in (has_before, has_after, has_earlier, has_later):
         greeted = greeted + there.astype(jnp.int32)
+    row = lax.broadcasted_iota(jnp.int32, (HALF, HALF), 0)
+    col = lax.broadcasted_iota(jnp.int32, (HALF, HALF), 1)
+    for level in range(masks_s.shape[0]):
+        wide = ((row >> (level + 1)) == (col >> (level + 1))) & (
+            ((row >> level) & 1) == 1
+        ) & (((col >> level) & 1) == 0)
+        masks_s[level] = wide.astype(f32).astype(bf16)
+
     pl.semaphore_wait(barrier, greeted)
 
     def rim_copies():
@@ -210,14 +220,6 @@
     @pl.when(jnp.logical_not(has_earlier))
     def _():
         recv_s[...] = jnp.zeros_like(recv_s)
-
-    row = lax.broadcasted_iota(jnp.int32, (HALF, HALF), 0)
-    col = lax.broadcasted_iota(jnp.int32, (HALF, HALF), 1)
-    for level in range(masks_s.shape[0]):
-        wide = ((row >> (level + 1)) == (col >> (level + 1))) & (
-            ((row >> level) & 1) == 1
-        ) & (((col >> level) & 1) == 0)
-        masks_s[level] = wide.astype(f32).astype(bf16)
 
     loads[0].wait()
     loads[1].wait()
@@ -324,16 +326,22 @@
             upper = lax.broadcasted_iota(jnp.int32, (NOTE, DK), 0) < NOTE // 2
             pair_s[parity, head, 2 * DK :, :] = jnp.where(upper, high.astype(f32), rest).astype(bf16)
             pair_copy(head).start()
-            attention = jnp.concatenate(
+            attention_s[head] = jnp.concatenate(
                 [
                     jnp.concatenate([d11 * qk[:HALF, :HALF], zero], axis=1),
                     jnp.concatenate([d21 * qk[HALF:, :HALF], d22 * qk[HALF:, HALF:]], axis=1),
                 ],
                 axis=0,
-            )
-            seen = dot(attention, solved)
+            ).astype(bf16)
+            solved_s[head] = solved
+            couple_s[head] = (e * q).astype(f32)
+
+    def attend(group):
+        for r in range(ratio):
+            head = group * ratio + r
+            seen = dot(attention_s[head], solved_s[head])
             local_s[head] = seen[:, :DK]
-            couple_s[head] = (e * q - seen[:, DK:]).astype(bf16)
+            couple_s[head] = couple_s[head] - seen[:, DK:]
 
     def unpacked(which, head):
         note = pair_s[which, head, 2 * DK :, :].astype(f32)
@@ -342,9 +350,8 @@
 
     def compose(group):
         for r in range(ratio):
-            pair_copy(group * ratio + r).wait_recv()
-        for r in range(ratio):
             head = group * ratio + r
+            pair_copy(head).wait_recv()
             end0, map0, inject0 = unpacked(0, head)
             end1, map1, inject1 = unpacked(1, head)
             both = dot(map1, jnp.concatenate([map0, inject0], axis=1))
@@ -353,25 +360,30 @@
             inject_s[head] = end1 * inject0.astype(f32) + inject1.astype(f32) - both[:, DK:]
             end_s[head] = jnp.broadcast_to(end1 * end0, (8, DK))
 
-    def relay(group):
+            @pl.when(has_later & jnp.logical_not(has_earlier))
+            def _(head=head):
+                send_s[head] = inject_s[head].astype(bf16)
+                state_copy(head).start()
+
+    def relay(group, waits):
         heads = [group * ratio + r for r in range(ratio)]
 
-        @pl.when(has_earlier)
-        def _():
-            for head in heads:
+        for head in heads:
+            if waits:
                 state_copy(head).wait_recv()
 
-        @pl.when(has_later)
-        def _():
-            for head in heads:
-                held = recv_s[head]
-                following = (
-                    end_s[head][0:1, :] * held.astype(f32)
-                    + inject_s[head]
-                    - dot(transit_s[head], held)
-                )
-                send_s[head] = following.astype(bf16)
-                state_copy(head).start()
+            if waits:
+
+                @pl.when(has_later)
+                def _(head=head):
+                    held = recv_s[head]
+                    following = (
+                        end_s[head][0:1, :] * held.astype(f32)
+                        + inject_s[head]
+                        - dot(transit_s[head], held)
+                    )
+                    send_s[head] = following.astype(bf16)
+                    state_copy(head).start()
 
         odd = parity == 1
         for head in heads:
@@ -390,15 +402,25 @@
         def _():
             local(turn)
 
-        @pl.when((turn >= 1) & (turn <= key_heads))
+        composing = (turn >= 1) & (turn <= key_heads)
+        group = turn - 1 - stage
+        relaying = (group >= 0) & (group < key_heads)
+
+        @pl.when(composing)
+        def _():
+            attend(turn - 1)
+
+        @pl.when(relaying & has_earlier)
+        def _():
+            relay(group, True)
+
+        @pl.when(composing)
         def _():
             compose(turn - 1)
 
-        group = turn - 1 - stage
-
-        @pl.when((group >= 0) & (group < key_heads))
+        @pl.when(relaying & jnp.logical_not(has_earlier))
         def _():
-            relay(group)
+            relay(group, False)
 
         return carry
 
@@ -507,7 +529,9 @@
             pltpu.VMEM((heads, DK, DK), bf16),
             pltpu.VMEM((heads, 8, DK), f32),
             pltpu.VMEM((heads, length, DK), f32),
-            pltpu.VMEM((heads, length, DK), bf16),
+            pltpu.VMEM((heads, length, DK), f32),
+            pltpu.VMEM((heads, length, length), bf16),
+            pltpu.VMEM((heads, length, 2 * DK), bf16),
             pltpu.VMEM((heads, DK, DK), bf16),
             pltpu.VMEM((heads, DK, DK), bf16),
             pltpu.VMEM((length, value_cols), bf16),

time: 45.2 us -> 43.8 us (0.969)
  Pallas kernels: 43.4 us -> 42 us
    pallas_call x1, Pallas kernels: 43.4 us -> 42 us  [shards(): pl.pallas_call(functools.partial(kernel, seq_count, head_count), out_shap...]
where the time goes in v3:
time: 43.8 us; the launch traced here: 43.7 us
  Pallas kernels  42 us (96%)
  local copies, waits for them, and re-layouts  1.67 us (4%)
    pallas_call x1, Pallas kernels, shards(): pl.pallas_call(functools.partial(kernel, seq_count, head_count), out_shap...  42 us
    unnamed x1, local copies, waits for them, and re-layouts  1.67 us

profile of v3, /device:TPU:29, one launch (start us, length us, event | category | flops | bytes accessed | tf_op | source)
XLA Modules:
  0.0 43.7 jit_solution(9613617991205644540)
XLA Ops:
  0.0 42.0 %shard_map.109 = bf16[64,2048]{1,0:T(8,128)(2,1)} custom-call(bf16[256,512]{1,0:T(8,128)(2,1)} %q_hbm.1, bf16[256,512]{1,0:T(8,128)(2,1)} %k_hbm.1, bf16[256,1024]{1,0:T(8,128)(2,1)} %v_hbm.1, bf16[256,1024]{1,0:T(8,128)(2,1)} %g_hbm.1, f32[8,256]{1,0:T(8,128)} %beta_hbm.1, f32[8,256]{1,0:T(8,128)} %decay_hbm.1, bf16[4,512]{1,0:T(4,128)(2,1)} %cq_hbm.1, ...), custom_call_target="tpu_custom_call" | custom-call | tf_op jit(solution)/shard_map/pallas_call | solution.py:512
  42.0 1.7 %copy.13 = bf16[64,2048]{1,0:T(8,128)(2,1)} copy(bf16[64,2048]{1,0:T(8,128)(2,1)} %shard_map.109) | data formatting | bytes 524288

commit v4 on v3

--- a/solution.py
+++ b/solution.py
@@ -14,7 +14,7 @@
 MESH = pl.DeviceIdType.MESH
 f32 = jnp.float32
 bf16 = jnp.bfloat16
-CHUNK = 512
+CHUNK = 256
 NOTE = 16
 
 

time: 43.8 us -> 43.8 us (level)
  no operation moved by 1% of the time
where the time goes in v4:
time: 43.8 us; the launch traced here: 43.6 us
  Pallas kernels  41.9 us (96%)
  local copies, waits for them, and re-layouts  1.67 us (4%)
    pallas_call x1, Pallas kernels, shards(): pl.pallas_call(functools.partial(kernel, seq_count, head_count), out_shap...  41.9 us
    unnamed x1, local copies, waits for them, and re-layouts  1.67 us

profile of v4, /device:TPU:29, one launch (start us, length us, event | category | flops | bytes accessed | tf_op | source)
XLA Modules:
  0.0 43.6 jit_solution(13222123086253280770)
XLA Ops:
  0.0 41.9 %shard_map.109 = bf16[64,2048]{1,0:T(8,128)(2,1)} custom-call(bf16[256,512]{1,0:T(8,128)(2,1)} %q_hbm.1, bf16[256,512]{1,0:T(8,128)(2,1)} %k_hbm.1, bf16[256,1024]{1,0:T(8,128)(2,1)} %v_hbm.1, bf16[256,1024]{1,0:T(8,128)(2,1)} %g_hbm.1, f32[8,256]{1,0:T(8,128)} %beta_hbm.1, f32[8,256]{1,0:T(8,128)} %decay_hbm.1, bf16[4,512]{1,0:T(4,128)(2,1)} %cq_hbm.1, ...), custom_call_target="tpu_custom_call" | custom-call | tf_op jit(solution)/shard_map/pallas_call | solution.py:512
  41.9 1.7 %copy.13 = bf16[64,2048]{1,0:T(8,128)(2,1)} copy(bf16[64,2048]{1,0:T(8,128)(2,1)} %shard_map.109) | data formatting | bytes 524288
